TPU v7x, 32 devices: a whole 2x2x4 slice. The times are simulated.
32 devices in a mesh: sub: 4 (over y, x), line: 8 (over z, core).
Axes of the slice: x: 2, y: 2, z: 4, core: 2. Of those that a mesh axis runs over, the one named last changes fastest.
Arguments:
- nodal_inverse: float32 [4, 128, 36864], P('sub', 'line'), may hold values from -1 to 1
- bus_source: float32 [4, 16, 12, 2048], P('sub', None, None, 'line'), may hold values from -16 to 16
- modal_map: float32 [12, 12], replicated, may hold values from -1.75 to 1.75
- admittance: float32 [4, 12, 2048], P('sub', None, 'line'), may hold values from 0.5 to 1.5
- attenuation: float32 [4, 12, 2048], P('sub', None, 'line'), may hold values from 0.6 to 0.95
- past_waves: float32 [4, 12, 12, 2048], P('sub', None, None, 'line'), may hold values from -6 to 6
- tie_code: int32 [8], P('line'), may hold values from 1 to 3, as said below
- travel_span: int32 [4, 2048], P('sub', 'line'), may hold values from 4 to 12, as said below
- bus_owner: int32 [4, 2048, 1], P('sub', 'line'), may hold values from 0 to 7; in each aligned block of 256 rows (0 to 255, 256 to 511, ..., all dimensions but the last counted through in order) at most 64 rows name the same one
- bus_local: int32 [4, 2048], P('sub', 'line'), may hold values from 0 to 255
- bus_count: int32 [4, 128], P('sub', 'line'), may hold values from 8 to 16
Outputs:
- volts: float32 [4, 16, 12, 2048], P('sub', None, None, 'line')
Inputs may be any that keep to these rules, and one draw needn't show every extreme that they name: Index s of the sub axis and index s XOR tie_code[l] are partners in column l. A line has the same travel time at both of its ends: travel_span[s, j] equals travel_span[partner(s, j), j]. `bus_owner`: among the 256 line ends of one device, at most 64 name the same owner.
All inputs are finite; a program needn't handle non-finite values.
Results may differ from a plain program's by a relative error of at most 0.0001.
Values sent between devices are 32-bit elements; how exact they have to be, the bound alone decides.
A program may use at most 64 MiB of HBM per device.

v0:
```python
import jax
import jax.numpy as jnp
from jax import lax
from jax.sharding import PartitionSpec as P

TMIN = 4


def solve_buses(nodal, right_side, live_bus, per_subset):
    subsets = nodal.shape[0]
    conductors = right_side.shape[0]
    node_count = conductors * per_subset
    square = nodal.reshape(subsets, node_count, node_count)
    stacked = jnp.transpose(
        (right_side * live_bus).reshape(conductors, subsets, per_subset), (1, 0, 2)
    ).reshape(subsets, node_count)
    solved = jnp.einsum("gij,gj->gi", square, stacked, precision=lax.Precision.HIGHEST)
    return (
        jnp.transpose(solved.reshape(subsets, conductors, per_subset), (1, 0, 2)).reshape(
            conductors, subsets * per_subset
        )
        * live_bus
    )


def per_device(
    nodal_inverse,
    bus_source,
    modal_map,
    admittance,
    attenuation,
    past_waves,
    tie_code,
    travel_span,
    bus_owner,
    bus_local,
    bus_count,
):
    highest = lax.Precision.HIGHEST
    nodal = nodal_inverse[0]
    source = bus_source[0]
    admit_here = admittance[0]
    damping = attenuation[0]
    initial = past_waves[0]
    spans_here = travel_span[0]
    owner_here = bus_owner[0, :, 0]
    local_here = bus_local[0]
    counts_here = bus_count[0]
    code_here = tie_code[0]
    conductors = admit_here.shape[0]
    line_count = admit_here.shape[1]
    steps_total = source.shape[0]
    bus_total = source.shape[2]
    subsets = nodal.shape[0]
    per_subset = bus_total // subsets
    depth_total = initial.shape[0]
    line_devices = lax.axis_size("line")
    capacity = 2 * line_count // line_devices
    live_bus = (
        (jnp.arange(per_subset, dtype=jnp.int32)[None, :] < counts_here[:, None])
        .astype(jnp.float32)
        .reshape(1, bus_total)
    )
    pick_table = (
        jnp.arange(depth_total, dtype=jnp.int32)[:, None] == (depth_total - spans_here)[None, :]
    ).astype(jnp.float32)[:, None, :]
    partner_index = jnp.bitwise_xor(lax.axis_index("sub"), code_here)
    owner_hot = (owner_here[:, None] == jnp.arange(line_devices, dtype=jnp.int32)[None, :]).astype(
        jnp.int32
    )
    earlier = jnp.cumsum(owner_hot, axis=0) - owner_hot
    position = jnp.sum(earlier * owner_hot, axis=1)
    slot_index = owner_here * capacity + position
    sent_ids = jnp.zeros((1, line_devices * capacity), jnp.int32).at[0, slot_index].set(local_here)
    landed_ids = lax.all_to_all(sent_ids, "line", split_axis=1, concat_axis=1, tiled=True)[0]

    def to_buses(inject):
        rows_here = inject.shape[0]
        slot_values = (
            jnp.zeros((rows_here, line_devices * capacity), jnp.float32)
            .at[:, slot_index]
            .set(inject)
        )
        landed = lax.all_to_all(slot_values, "line", split_axis=1, concat_axis=1, tiled=True)
        return jnp.zeros((rows_here, bus_total), jnp.float32).at[:, landed_ids].add(landed)

    def to_lines(voltage):
        returned = lax.all_to_all(
            voltage[:, landed_ids], "line", split_axis=1, concat_axis=1, tiled=True
        )
        return returned[:, slot_index]

    def send_each(timeline, outgoing, instant):
        everyone = lax.all_gather(outgoing[None], "sub", axis=0, tiled=True)
        arrived = lax.dynamic_index_in_dim(everyone, partner_index, 0, keepdims=False)
        return lax.dynamic_update_index_in_dim(timeline, arrived, depth_total + instant, 0)

    def history_at(timeline, instant):
        window = lax.dynamic_slice_in_dim(timeline, instant, depth_total, 0)
        return damping * jnp.sum(window * pick_table, axis=0)

    timeline = jnp.concatenate(
        [initial, jnp.zeros((steps_total, conductors, line_count), jnp.float32)], axis=0
    )
    volt_record = jnp.zeros((steps_total, conductors, bus_total), jnp.float32)

    def one_block(block_number, carried):
        timeline, volt_record = carried
        histories = []
        injects = []
        for inner in range(TMIN):
            instant = block_number * TMIN + inner
            history = history_at(timeline, instant)
            histories.append(history)
            injects.append(jnp.dot(modal_map, history, precision=highest))
        summed = to_buses(jnp.concatenate(injects, axis=0)).reshape(TMIN, conductors, bus_total)
        voltages = []
        for inner in range(TMIN):
            instant = block_number * TMIN + inner
            right_side = (
                lax.dynamic_index_in_dim(source, instant, 0, keepdims=False) + summed[inner]
            )
            voltage = solve_buses(nodal, right_side, live_bus, per_subset)
            volt_record = lax.dynamic_update_index_in_dim(volt_record, voltage, instant, 0)
            voltages.append(voltage)
        at_lines = to_lines(jnp.concatenate(voltages, axis=0)).reshape(TMIN, conductors, line_count)
        for inner in range(TMIN):
            instant = block_number * TMIN + inner
            modal_volts = jnp.dot(modal_map.T, at_lines[inner], precision=highest)
            outgoing = 2.0 * admit_here * modal_volts - histories[inner]
            timeline = send_each(timeline, outgoing, instant)
        return (timeline, volt_record)

    timeline, volt_record = lax.fori_loop(
        0, steps_total // TMIN, one_block, (timeline, volt_record)
    )
    return volt_record[None]


def solution(mesh):
    in_specs = (
        P("sub", "line", None),
        P("sub", None, None, "line"),
        P(),
        P("sub", None, "line"),
        P("sub", None, "line"),
        P("sub", None, None, "line"),
        P("line"),
        P("sub", "line"),
        P("sub", "line", None),
        P("sub", "line"),
        P("sub", "line"),
    )
    out_specs = P("sub", None, None, "line")
    return jax.shard_map(
        per_device, mesh=mesh, in_specs=in_specs, out_specs=out_specs, check_vma=False
    )
```

profile of v0, /device:TPU:0, one launch (start us, length us, event | category | flops | bytes accessed | tf_op | source)
XLA Modules:
  0.0 439.7 jit_solution(1715135332556245998)
XLA Ops:
  7.8 6.3 %all-to-all-start.2 = ((s32[1,8,64]{2,0,1:T(1,128)}), s32[1,8,64]{2,0,1:T(1,128)S(1)}, u32[]{:S(2)}, u32[]{:S(2)}) async-start(s32[1,8,64]{2,0,1:T(1,128)} %all_to_all.42), calls=%async_computation.2 | async-start | bytes 8192 | tf_op jit(solution)/shard_map/all_to_all | solution.py:75
  22.2 415.8 %while.20 = (s32[]{:T(128)}, f32[28,12,256]{2,1,0:T(8,128)}, f32[16,12,256]{2,1,0:T(8,128)}, f32[12,256]{1,0:T(8,128)S(1)}, f32[16,12,256]{2,1,0:T(8,128)}, /*in...) while((s32[]{:T(128)}, f32[28,12,256]{2,1,0:T(8,128)}, ...), condition=%wide.region_11.12_spmd.clone, body=%wide.region_4.11_spmd.clone.sunk | while | flops 32340764 | bytes 21557844 | solution.py:134
  31.3 5.0 %all-to-all-start = ((f32[8,1,3072]{2,1,0:T(1,128)}), f32[8,1,3072]{2,1,0:T(1,128)S(1)}, u32[]{:S(2)}, u32[]{:S(2)}) async-start(f32[8,1,3072]{2,1,0:T(1,128)} %reshape.879), calls=%async_computation | async-start | bytes 196608 | tf_op jit(solution)/shard_map/while/body/eval_jaxpr/all_to_all | solution.py:84
  42.1 2.7 reshape_squeeze.18
  48.5 3.9 scatter_custom_fusion.15
  59.8 2.7 fusion.123
  64.5 2.7 fusion.122
  69.2 2.7 fusion.124
  73.0 2.7 fusion.125
  79.0 4.5 %all-to-all-start.1 = ((f32[8,1,3072]{2,1,0:T(1,128)}), f32[8,1,3072]{2,1,0:T(1,128)S(1)}, u32[]{:S(2)}, u32[]{:S(2)}) async-start(f32[8,1,3072]{2,1,0:T(1,128)} %reshape.894), calls=%async_computation.1 | async-start | bytes 196608 | tf_op jit(solution)/shard_map/while/body/eval_jaxpr/all_to_all | solution.py:88
  85.9 3.9 all-to-all-done.1
  93.6 8.3 %all-gather.16 = f32[4,12,256]{2,1,0:T(8,128)S(1)} all-gather(f32[1,12,256]{2,1,0:T(8,128)S(1)} %fusion.126), channel_id=2, replica_groups=mesh['sub'=4,'line'=8] {'sub'}, dimensions={0}, use_global_device_ids=true | all-gather | bytes 61440 | tf_op jit(solution)/shard_map/while/body/eval_jaxpr/all_gather | solution.py:94
  101.9 8.4 %all-gather.17 = f32[4,12,256]{2,1,0:T(8,128)S(1)} all-gather(f32[1,12,256]{2,1,0:T(8,128)S(1)} %fusion.127), channel_id=3, replica_groups=mesh['sub'=4,'line'=8] {'sub'}, dimensions={0}, use_global_device_ids=true | all-gather | bytes 61440 | tf_op jit(solution)/shard_map/while/body/eval_jaxpr/all_gather | solution.py:94
  110.3 7.3 %all-gather.18 = f32[4,12,256]{2,1,0:T(8,128)S(1)} all-gather(f32[1,12,256]{2,1,0:T(8,128)S(1)} %fusion.128), channel_id=4, replica_groups=mesh['sub'=4,'line'=8] {'sub'}, dimensions={0}, use_global_device_ids=true | all-gather | bytes 61440 | tf_op jit(solution)/shard_map/while/body/eval_jaxpr/all_gather | solution.py:94
  117.6 8.1 %all-gather.19 = f32[4,12,256]{2,1,0:T(8,128)S(1)} all-gather(f32[1,12,256]{2,1,0:T(8,128)S(1)} %fusion.129), channel_id=5, replica_groups=mesh['sub'=4,'line'=8] {'sub'}, dimensions={0}, use_global_device_ids=true | all-gather | bytes 61440 | tf_op jit(solution)/shard_map/while/body/eval_jaxpr/all_gather | solution.py:94
  137.3 3.4 all-to-all-start
  146.5 2.7 reshape_squeeze.18
  152.9 3.9 scatter_custom_fusion.15
  164.1 2.7 fusion.123
  168.8 2.7 fusion.122
  173.5 2.7 fusion.124
  177.4 2.7 fusion.125
  183.4 4.3 all-to-all-start.1
  190.1 3.9 all-to-all-done.1
  197.8 7.4 %all-gather.16 = f32[4,12,256]{2,1,0:T(8,128)S(1)} all-gather(f32[1,12,256]{2,1,0:T(8,128)S(1)} %fusion.126), channel_id=2, replica_groups=mesh['sub'=4,'line'=8] {'sub'}, dimensions={0}, use_global_device_ids=true | all-gather | bytes 61440 | tf_op jit(solution)/shard_map/while/body/eval_jaxpr/all_gather | solution.py:94
  205.2 8.3 %all-gather.17 = f32[4,12,256]{2,1,0:T(8,128)S(1)} all-gather(f32[1,12,256]{2,1,0:T(8,128)S(1)} %fusion.127), channel_id=3, replica_groups=mesh['sub'=4,'line'=8] {'sub'}, dimensions={0}, use_global_device_ids=true | all-gather | bytes 61440 | tf_op jit(solution)/shard_map/while/body/eval_jaxpr/all_gather | solution.py:94
  213.6 7.3 %all-gather.18 = f32[4,12,256]{2,1,0:T(8,128)S(1)} all-gather(f32[1,12,256]{2,1,0:T(8,128)S(1)} %fusion.128), channel_id=4, replica_groups=mesh['sub'=4,'line'=8] {'sub'}, dimensions={0}, use_global_device_ids=true | all-gather | bytes 61440 | tf_op jit(solution)/shard_map/while/body/eval_jaxpr/all_gather | solution.py:94
  220.9 8.2 %all-gather.19 = f32[4,12,256]{2,1,0:T(8,128)S(1)} all-gather(f32[1,12,256]{2,1,0:T(8,128)S(1)} %fusion.129), channel_id=5, replica_groups=mesh['sub'=4,'line'=8] {'sub'}, dimensions={0}, use_global_device_ids=true | all-gather | bytes 61440 | tf_op jit(solution)/shard_map/while/body/eval_jaxpr/all_gather | solution.py:94
  240.6 3.4 all-to-all-start
  249.7 2.7 reshape_squeeze.18
  256.2 3.9 scatter_custom_fusion.15
  267.4 2.7 fusion.123
  272.1 2.7 fusion.122
  286.7 4.3 all-to-all-start.1
  293.4 3.9 all-to-all-done.1
  301.1 7.4 %all-gather.16 = f32[4,12,256]{2,1,0:T(8,128)S(1)} all-gather(f32[1,12,256]{2,1,0:T(8,128)S(1)} %fusion.126), channel_id=2, replica_groups=mesh['sub'=4,'line'=8] {'sub'}, dimensions={0}, use_global_device_ids=true | all-gather | bytes 61440 | tf_op jit(solution)/shard_map/while/body/eval_jaxpr/all_gather | solution.py:94
  308.5 8.3 %all-gather.17 = f32[4,12,256]{2,1,0:T(8,128)S(1)} all-gather(f32[1,12,256]{2,1,0:T(8,128)S(1)} %fusion.127), channel_id=3, replica_groups=mesh['sub'=4,'line'=8] {'sub'}, dimensions={0}, use_global_device_ids=true | all-gather | bytes 61440 | tf_op jit(solution)/shard_map/while/body/eval_jaxpr/all_gather | solution.py:94
  316.8 7.3 %all-gather.18 = f32[4,12,256]{2,1,0:T(8,128)S(1)} all-gather(f32[1,12,256]{2,1,0:T(8,128)S(1)} %fusion.128), channel_id=4, replica_groups=mesh['sub'=4,'line'=8] {'sub'}, dimensions={0}, use_global_device_ids=true | all-gather | bytes 61440 | tf_op jit(solution)/shard_map/while/body/eval_jaxpr/all_gather | solution.py:94
  324.1 8.2 %all-gather.19 = f32[4,12,256]{2,1,0:T(8,128)S(1)} all-gather(f32[1,12,256]{2,1,0:T(8,128)S(1)} %fusion.129), channel_id=5, replica_groups=mesh['sub'=4,'line'=8] {'sub'}, dimensions={0}, use_global_device_ids=true | all-gather | bytes 61440 | tf_op jit(solution)/shard_map/while/body/eval_jaxpr/all_gather | solution.py:94
  343.8 3.4 all-to-all-start
  353.0 2.7 reshape_squeeze.18
  359.5 3.9 scatter_custom_fusion.15
  390.0 4.3 all-to-all-start.1
  396.7 3.9 all-to-all-done.1
  404.4 7.4 %all-gather.16 = f32[4,12,256]{2,1,0:T(8,128)S(1)} all-gather(f32[1,12,256]{2,1,0:T(8,128)S(1)} %fusion.126), channel_id=2, replica_groups=mesh['sub'=4,'line'=8] {'sub'}, dimensions={0}, use_global_device_ids=true | all-gather | bytes 61440 | tf_op jit(solution)/shard_map/while/body/eval_jaxpr/all_gather | solution.py:94
  411.8 8.3 %all-gather.17 = f32[4,12,256]{2,1,0:T(8,128)S(1)} all-gather(f32[1,12,256]{2,1,0:T(8,128)S(1)} %fusion.127), channel_id=3, replica_groups=mesh['sub'=4,'line'=8] {'sub'}, dimensions={0}, use_global_device_ids=true | all-gather | bytes 61440 | tf_op jit(solution)/shard_map/while/body/eval_jaxpr/all_gather | solution.py:94
  420.1 7.3 %all-gather.18 = f32[4,12,256]{2,1,0:T(8,128)S(1)} all-gather(f32[1,12,256]{2,1,0:T(8,128)S(1)} %fusion.128), channel_id=4, replica_groups=mesh['sub'=4,'line'=8] {'sub'}, dimensions={0}, use_global_device_ids=true | all-gather | bytes 61440 | tf_op jit(solution)/shard_map/while/body/eval_jaxpr/all_gather | solution.py:94
  427.4 8.2 %all-gather.19 = f32[4,12,256]{2,1,0:T(8,128)S(1)} all-gather(f32[1,12,256]{2,1,0:T(8,128)S(1)} %fusion.129), channel_id=5, replica_groups=mesh['sub'=4,'line'=8] {'sub'}, dimensions={0}, use_global_device_ids=true | all-gather | bytes 61440 | tf_op jit(solution)/shard_map/while/body/eval_jaxpr/all_gather | solution.py:94
  (479 shorter events, 203.4 us)
Async XLA Ops:
  7.8 11.8 %all-to-all-start.2 = ((s32[1,8,64]{2,0,1:T(1,128)}), s32[1,8,64]{2,0,1:T(1,128)S(1)}, u32[]{:S(2)}, u32[]{:S(2)}) async-start(s32[1,8,64]{2,0,1:T(1,128)} %all_to_all.42), calls=%async_computation.2 | async-start | bytes 8192 | tf_op jit(solution)/shard_map/all_to_all | solution.py:75
  31.3 14.7 %all-to-all-start = ((f32[8,1,3072]{2,1,0:T(1,128)}), f32[8,1,3072]{2,1,0:T(1,128)S(1)}, u32[]{:S(2)}, u32[]{:S(2)}) async-start(f32[8,1,3072]{2,1,0:T(1,128)} %reshape.879), calls=%async_computation | async-start | bytes 196608 | tf_op jit(solution)/shard_map/while/body/eval_jaxpr/all_to_all | solution.py:84
  37.0 9.5 %copy-start.12 = (s32[512,1]{0,1:T(1,128)}, s32[512,1]{0,1:T(1,128)S(1)}, u32[]{:S(2)}) copy-start(s32[512,1]{0,1:T(1,128)S(1)} %compare_select_fusion.5) | copy-start | bytes 6148 | tf_op jit(solution)/shard_map/while
  37.8 8.8 %copy-start.9 = (f32[16,16]{1,0:T(8,128)}, f32[16,16]{1,0:T(8,128)S(1)}, u32[]{:S(2)}) copy-start(f32[16,16]{1,0:T(8,128)S(1)} %fusion.121) | copy-start | bytes 3076 | tf_op jit(solution)/shard_map/while
  72.9 10.6 %copy-start.11 = (f32[256]{0:T(256)S(1)}, f32[256]{0:T(256)}, u32[]{:S(2)}) copy-start(f32[256]{0:T(256)} %mul.650) | copy-start | bytes 3076 | tf_op jit(solution)/shard_map/while
  73.0 19.3 %copy-start = (f32[12,12]{1,0:T(8,128)S(1)}, f32[12,12]{1,0:T(8,128)}, u32[]{:S(2)}) copy-start(f32[12,12]{1,0:T(8,128)} %get-tuple-element.715) | copy-start | bytes 1732 | tf_op jit(solution)/shard_map/while
  73.0 19.3 %copy-start.8 = (f32[12,256]{1,0:T(8,128)S(1)}, f32[12,256]{1,0:T(8,128)}, u32[]{:S(2)}) copy-start(f32[12,256]{1,0:T(8,128)} %copy-done.7) | copy-start | bytes 36868 | tf_op jit(solution)/shard_map/while
  73.0 19.7 %copy-start.6 = (f32[12,256]{1,0:T(8,128)S(1)}, f32[12,256]{1,0:T(8,128)}, u32[]{:S(2)}) copy-start(f32[12,256]{1,0:T(8,128)} %copy-done.5) | copy-start | bytes 36868 | tf_op jit(solution)/shard_map/while
  75.7 17.3 %copy-start.4 = (f32[12,256]{1,0:T(8,128)S(1)}, f32[12,256]{1,0:T(8,128)}, u32[]{:S(2)}) copy-start(f32[12,256]{1,0:T(8,128)} %copy-done.3) | copy-start | bytes 36868 | tf_op jit(solution)/shard_map/while
  75.7 17.6 %copy-start.2 = (f32[12,256]{1,0:T(8,128)S(1)}, f32[12,256]{1,0:T(8,128)}, u32[]{:S(2)}) copy-start(f32[12,256]{1,0:T(8,128)} %copy-done.1) | copy-start | bytes 36868 | tf_op jit(solution)/shard_map/while
  79.0 10.8 %all-to-all-start.1 = ((f32[8,1,3072]{2,1,0:T(1,128)}), f32[8,1,3072]{2,1,0:T(1,128)S(1)}, u32[]{:S(2)}, u32[]{:S(2)}) async-start(f32[8,1,3072]{2,1,0:T(1,128)} %reshape.894), calls=%async_computation.1 | async-start | bytes 196608 | tf_op jit(solution)/shard_map/while/body/eval_jaxpr/all_to_all | solution.py:88
  131.6 3.4 copy-start.3
  131.6 3.4 copy-start.5
  131.6 3.4 copy-start.7
  137.3 13.1 %all-to-all-start = ((f32[8,1,3072]{2,1,0:T(1,128)}), f32[8,1,3072]{2,1,0:T(1,128)S(1)}, u32[]{:S(2)}, u32[]{:S(2)}) async-start(f32[8,1,3072]{2,1,0:T(1,128)} %reshape.879), calls=%async_computation | async-start | bytes 196608 | tf_op jit(solution)/shard_map/while/body/eval_jaxpr/all_to_all | solution.py:84
  141.4 9.5 %copy-start.12 = (s32[512,1]{0,1:T(1,128)}, s32[512,1]{0,1:T(1,128)S(1)}, u32[]{:S(2)}) copy-start(s32[512,1]{0,1:T(1,128)S(1)} %compare_select_fusion.5) | copy-start | bytes 6148 | tf_op jit(solution)/shard_map/while
  142.1 8.8 %copy-start.9 = (f32[16,16]{1,0:T(8,128)}, f32[16,16]{1,0:T(8,128)S(1)}, u32[]{:S(2)}) copy-start(f32[16,16]{1,0:T(8,128)S(1)} %fusion.121) | copy-start | bytes 3076 | tf_op jit(solution)/shard_map/while
  177.2 10.5 %copy-start.11 = (f32[256]{0:T(256)S(1)}, f32[256]{0:T(256)}, u32[]{:S(2)}) copy-start(f32[256]{0:T(256)} %mul.650) | copy-start | bytes 3076 | tf_op jit(solution)/shard_map/while
  177.3 19.2 %copy-start = (f32[12,12]{1,0:T(8,128)S(1)}, f32[12,12]{1,0:T(8,128)}, u32[]{:S(2)}) copy-start(f32[12,12]{1,0:T(8,128)} %get-tuple-element.715) | copy-start | bytes 1732 | tf_op jit(solution)/shard_map/while
  177.3 19.2 %copy-start.8 = (f32[12,256]{1,0:T(8,128)S(1)}, f32[12,256]{1,0:T(8,128)}, u32[]{:S(2)}) copy-start(f32[12,256]{1,0:T(8,128)} %copy-done.7) | copy-start | bytes 36868 | tf_op jit(solution)/shard_map/while
  177.4 19.5 %copy-start.6 = (f32[12,256]{1,0:T(8,128)S(1)}, f32[12,256]{1,0:T(8,128)}, u32[]{:S(2)}) copy-start(f32[12,256]{1,0:T(8,128)} %copy-done.5) | copy-start | bytes 36868 | tf_op jit(solution)/shard_map/while
  180.0 17.2 %copy-start.4 = (f32[12,256]{1,0:T(8,128)S(1)}, f32[12,256]{1,0:T(8,128)}, u32[]{:S(2)}) copy-start(f32[12,256]{1,0:T(8,128)} %copy-done.3) | copy-start | bytes 36868 | tf_op jit(solution)/shard_map/while
  180.1 17.5 %copy-start.2 = (f32[12,256]{1,0:T(8,128)S(1)}, f32[12,256]{1,0:T(8,128)}, u32[]{:S(2)}) copy-start(f32[12,256]{1,0:T(8,128)} %copy-done.1) | copy-start | bytes 36868 | tf_op jit(solution)/shard_map/while
  183.4 10.7 %all-to-all-start.1 = ((f32[8,1,3072]{2,1,0:T(1,128)}), f32[8,1,3072]{2,1,0:T(1,128)S(1)}, u32[]{:S(2)}, u32[]{:S(2)}) async-start(f32[8,1,3072]{2,1,0:T(1,128)} %reshape.894), calls=%async_computation.1 | async-start | bytes 196608 | tf_op jit(solution)/shard_map/while/body/eval_jaxpr/all_to_all | solution.py:88
  234.9 3.4 copy-start.3
  240.6 13.1 %all-to-all-start = ((f32[8,1,3072]{2,1,0:T(1,128)}), f32[8,1,3072]{2,1,0:T(1,128)S(1)}, u32[]{:S(2)}, u32[]{:S(2)}) async-start(f32[8,1,3072]{2,1,0:T(1,128)} %reshape.879), calls=%async_computation | async-start | bytes 196608 | tf_op jit(solution)/shard_map/while/body/eval_jaxpr/all_to_all | solution.py:84
  244.7 9.5 %copy-start.12 = (s32[512,1]{0,1:T(1,128)}, s32[512,1]{0,1:T(1,128)S(1)}, u32[]{:S(2)}) copy-start(s32[512,1]{0,1:T(1,128)S(1)} %compare_select_fusion.5) | copy-start | bytes 6148 | tf_op jit(solution)/shard_map/while
  245.4 8.8 %copy-start.9 = (f32[16,16]{1,0:T(8,128)}, f32[16,16]{1,0:T(8,128)S(1)}, u32[]{:S(2)}) copy-start(f32[16,16]{1,0:T(8,128)S(1)} %fusion.121) | copy-start | bytes 3076 | tf_op jit(solution)/shard_map/while
  280.5 10.5 %copy-start.11 = (f32[256]{0:T(256)S(1)}, f32[256]{0:T(256)}, u32[]{:S(2)}) copy-start(f32[256]{0:T(256)} %mul.650) | copy-start | bytes 3076 | tf_op jit(solution)/shard_map/while
  280.6 19.2 %copy-start = (f32[12,12]{1,0:T(8,128)S(1)}, f32[12,12]{1,0:T(8,128)}, u32[]{:S(2)}) copy-start(f32[12,12]{1,0:T(8,128)} %get-tuple-element.715) | copy-start | bytes 1732 | tf_op jit(solution)/shard_map/while
  280.6 19.2 %copy-start.8 = (f32[12,256]{1,0:T(8,128)S(1)}, f32[12,256]{1,0:T(8,128)}, u32[]{:S(2)}) copy-start(f32[12,256]{1,0:T(8,128)} %copy-done.7) | copy-start | bytes 36868 | tf_op jit(solution)/shard_map/while
  280.6 19.5 %copy-start.6 = (f32[12,256]{1,0:T(8,128)S(1)}, f32[12,256]{1,0:T(8,128)}, u32[]{:S(2)}) copy-start(f32[12,256]{1,0:T(8,128)} %copy-done.5) | copy-start | bytes 36868 | tf_op jit(solution)/shard_map/while
  283.3 17.2 %copy-start.4 = (f32[12,256]{1,0:T(8,128)S(1)}, f32[12,256]{1,0:T(8,128)}, u32[]{:S(2)}) copy-start(f32[12,256]{1,0:T(8,128)} %copy-done.3) | copy-start | bytes 36868 | tf_op jit(solution)/shard_map/while
  283.3 17.5 %copy-start.2 = (f32[12,256]{1,0:T(8,128)S(1)}, f32[12,256]{1,0:T(8,128)}, u32[]{:S(2)}) copy-start(f32[12,256]{1,0:T(8,128)} %copy-done.1) | copy-start | bytes 36868 | tf_op jit(solution)/shard_map/while
  286.7 10.7 %all-to-all-start.1 = ((f32[8,1,3072]{2,1,0:T(1,128)}), f32[8,1,3072]{2,1,0:T(1,128)S(1)}, u32[]{:S(2)}, u32[]{:S(2)}) async-start(f32[8,1,3072]{2,1,0:T(1,128)} %reshape.894), calls=%async_computation.1 | async-start | bytes 196608 | tf_op jit(solution)/shard_map/while/body/eval_jaxpr/all_to_all | solution.py:88
  338.1 3.4 copy-start.3
  338.1 3.4 copy-start.5
  338.1 3.4 copy-start.7
  343.8 13.1 %all-to-all-start = ((f32[8,1,3072]{2,1,0:T(1,128)}), f32[8,1,3072]{2,1,0:T(1,128)S(1)}, u32[]{:S(2)}, u32[]{:S(2)}) async-start(f32[8,1,3072]{2,1,0:T(1,128)} %reshape.879), calls=%async_computation | async-start | bytes 196608 | tf_op jit(solution)/shard_map/while/body/eval_jaxpr/all_to_all | solution.py:84
  347.9 9.5 %copy-start.12 = (s32[512,1]{0,1:T(1,128)}, s32[512,1]{0,1:T(1,128)S(1)}, u32[]{:S(2)}) copy-start(s32[512,1]{0,1:T(1,128)S(1)} %compare_select_fusion.5) | copy-start | bytes 6148 | tf_op jit(solution)/shard_map/while
  348.7 8.8 %copy-start.9 = (f32[16,16]{1,0:T(8,128)}, f32[16,16]{1,0:T(8,128)S(1)}, u32[]{:S(2)}) copy-start(f32[16,16]{1,0:T(8,128)S(1)} %fusion.121) | copy-start | bytes 3076 | tf_op jit(solution)/shard_map/while
  383.8 10.5 %copy-start.11 = (f32[256]{0:T(256)S(1)}, f32[256]{0:T(256)}, u32[]{:S(2)}) copy-start(f32[256]{0:T(256)} %mul.650) | copy-start | bytes 3076 | tf_op jit(solution)/shard_map/while
  383.9 19.2 %copy-start = (f32[12,12]{1,0:T(8,128)S(1)}, f32[12,12]{1,0:T(8,128)}, u32[]{:S(2)}) copy-start(f32[12,12]{1,0:T(8,128)} %get-tuple-element.715) | copy-start | bytes 1732 | tf_op jit(solution)/shard_map/while
  383.9 19.2 %copy-start.8 = (f32[12,256]{1,0:T(8,128)S(1)}, f32[12,256]{1,0:T(8,128)}, u32[]{:S(2)}) copy-start(f32[12,256]{1,0:T(8,128)} %copy-done.7) | copy-start | bytes 36868 | tf_op jit(solution)/shard_map/while
  383.9 19.5 %copy-start.6 = (f32[12,256]{1,0:T(8,128)S(1)}, f32[12,256]{1,0:T(8,128)}, u32[]{:S(2)}) copy-start(f32[12,256]{1,0:T(8,128)} %copy-done.5) | copy-start | bytes 36868 | tf_op jit(solution)/shard_map/while
  386.6 17.2 %copy-start.4 = (f32[12,256]{1,0:T(8,128)S(1)}, f32[12,256]{1,0:T(8,128)}, u32[]{:S(2)}) copy-start(f32[12,256]{1,0:T(8,128)} %copy-done.3) | copy-start | bytes 36868 | tf_op jit(solution)/shard_map/while
  386.6 17.5 %copy-start.2 = (f32[12,256]{1,0:T(8,128)S(1)}, f32[12,256]{1,0:T(8,128)}, u32[]{:S(2)}) copy-start(f32[12,256]{1,0:T(8,128)} %copy-done.1) | copy-start | bytes 36868 | tf_op jit(solution)/shard_map/while
  390.0 10.7 %all-to-all-start.1 = ((f32[8,1,3072]{2,1,0:T(1,128)}), f32[8,1,3072]{2,1,0:T(1,128)S(1)}, u32[]{:S(2)}, u32[]{:S(2)}) async-start(f32[8,1,3072]{2,1,0:T(1,128)} %reshape.894), calls=%async_computation.1 | async-start | bytes 196608 | tf_op jit(solution)/shard_map/while/body/eval_jaxpr/all_to_all | solution.py:88
  (13 other events, 40.4 us)
where the time goes:
time: 444 us; the launch traced here: 440 us
  blocking collectives  126 us (28%)
  local copies, waits for them, and re-layouts  123 us (28%)
  other arithmetic  73.1 us (16%)
  matrix products  61.1 us (14%)
  starting transfers between devices  38.9 us (9%)
  waiting for transfers between devices  15.8 us (4%)
    all_gather x16, blocking collectives, send_each(): everyone = lax.all_gather(outgoing[None], 'sub', axis=0, tiled=True)  126 us
    dot_general x16, matrix products, solve_buses(): jnp.einsum('gij,gj->gi', square, stacked, precision=lax.Precision.HIGHEST)  42.9 us
    squeeze x16, local copies, waits for them, and re-layouts, one_block(): summed[inner]  17.6 us
    all_to_all x4, starting transfers between devices, to_lines(): lax.all_to_all(voltage[:, landed_ids], 'line', split_axis=1, concat_axis=...  17.5 us
    scatter-add x4, other arithmetic, to_buses(): jnp.zeros((rows_here, bus_total), jnp.float32).at[:, landed_ids].add(landed)  15.7 us
    all_to_all x4, waiting for transfers between devices, to_lines(): lax.all_to_all(voltage[:, landed_ids], 'line', split_axis=1, concat_axis=...  15.7 us
    all_to_all x4, starting transfers between devices, to_buses(): lax.all_to_all(slot_values, 'line', split_axis=1, concat_axis=1, tiled=True)  15.1 us
    dot_general x16, matrix products, one_block(): injects.append(jnp.dot(modal_map, history, precision=highest))  13.4 us
  transfers between devices with their start and end apart: 9, of which 5 were waited for; matrix products, arithmetic and copies ran while one was open for 12% of the time, Pallas kernels for 0%

commit v1 on v0

v1 whole, which is shorter than its diff:
```python
import functools

import jax
import jax.numpy as jnp
from jax import lax
from jax.experimental import pallas as pl
from jax.experimental.pallas import tpu as pltpu
from jax.sharding import PartitionSpec as P

TMIN = 4
PAD = 16
ROWS = TMIN * PAD
BF = jnp.bfloat16
F32 = jnp.float32
MESH = pl.DeviceIdType.MESH


def split(x):
    high = x.astype(BF)
    return high, (x - high.astype(F32)).astype(BF)


def mm(a, b):
    return jnp.dot(a, b, preferred_element_type=F32)


def pick(x, hot):
    high, low = split(x)
    both = mm(jnp.concatenate([high, low], axis=0), hot)
    return both[: x.shape[0]] + both[x.shape[0] :]


def apply_map(cat, x):
    high, low = split(x)
    return mm(cat, jnp.concatenate([high, high, low], axis=0))


def iota(shape, axis):
    return lax.broadcasted_iota(jnp.int32, shape, axis)


def kernel(
    n_line, n_sub, w_hbm, src, mmap, adm, att, past, code, span, owner, local, counts, out,
    w_flat, w_split, timeline, p_hot, pt_hot, q_hot, qt_hot, spread, map_cat, mapt_cat,
    source, admit, hist, inj_send, inj_recv, v_send, v_recv, sub_send, sub_recv,
    w_sem, inj_ss, inj_rs, v_ss, v_rs, sub_ss, sub_rs,
):
    me = lax.axis_index("line")
    grp = lax.axis_index("sub")
    steps, cond, buses = src.shape[1:]
    lines = adm.shape[2]
    depth = past.shape[1]
    subsets = w_hbm.shape[1]
    per = buses // subsets
    nodes = cond * per
    blocks = steps // TMIN
    cap = 2 * lines // n_line
    slots = n_line * cap
    parts = 128 // cap
    prow = ROWS // parts

    barrier = pltpu.get_barrier_semaphore()
    for k in range(1, n_line):
        pl.semaphore_signal(
            barrier, inc=1, device_id={"line": lax.rem(me + k, n_line)}, device_id_type=MESH
        )
    for k in range(1, n_sub):
        pl.semaphore_signal(
            barrier, inc=1, device_id={"sub": lax.rem(grp + k, n_sub)}, device_id_type=MESH
        )
    w_copy = pltpu.make_async_copy(w_hbm.at[0], w_flat, w_sem)
    w_copy.start()

    def line_copy(send, recv, ss, rs, k):
        to = lax.rem(me + k, n_line)
        return pltpu.make_async_remote_copy(
            src_ref=send.at[to], dst_ref=recv.at[me], send_sem=ss.at[k], recv_sem=rs.at[k],
            device_id={"line": to}, device_id_type=MESH,
        )

    def line_wait(send, recv, ss, rs):
        for k in range(1, n_line):
            frm = lax.rem(me + n_line - k, n_line)
            pltpu.make_async_remote_copy(
                src_ref=send.at[frm], dst_ref=recv.at[frm], send_sem=ss.at[k], recv_sem=rs.at[k],
                device_id={"line": frm}, device_id_type=MESH,
            ).wait_recv()
        for k in range(1, n_line):
            line_copy(send, recv, ss, rs, k).wait_send()

    def pack(x, send, recv):
        for d in range(n_line):
            send[d] = jnp.concatenate(
                [x[g * prow : (g + 1) * prow, d * cap : (d + 1) * cap] for g in range(parts)], axis=1
            )
        recv[me] = send[me]

    def unpack(recv):
        return jnp.concatenate(
            [
                jnp.concatenate(
                    [recv[d][:, g * cap : (g + 1) * cap] for d in range(n_line)], axis=1
                )
                for g in range(parts)
            ],
            axis=0,
        )

    def sub_copy(parity, k):
        return pltpu.make_async_remote_copy(
            src_ref=sub_send, dst_ref=sub_recv.at[parity, k - 1],
            send_sem=sub_ss.at[parity, k - 1], recv_sem=sub_rs.at[parity, k - 1],
            device_id={"sub": lax.rem(grp + k, n_sub)}, device_id_type=MESH,
        )

    hot_t = (iota((PAD, lines), 0) == owner[...]).astype(F32)
    upper = (iota((lines, lines), 0) < iota((lines, lines), 1)).astype(F32).astype(BF)
    earlier = mm(hot_t.astype(BF), upper)
    base = (iota((PAD, lines), 0) * cap).astype(F32)
    slot_row = jnp.sum(hot_t * (base + earlier), axis=0, keepdims=True).astype(jnp.int32)
    pt = (iota((slots, lines), 0) == slot_row).astype(F32)
    pt_hot[...] = pt.astype(BF)
    p_hot[...] = pt.T.astype(BF)

    stretch = ((iota((ROWS, cond), 0) & (PAD - 1)) == iota((ROWS, cond), 1)).astype(F32)
    same = (iota((ROWS, ROWS), 0) // PAD == iota((ROWS, ROWS), 1) // PAD).astype(F32)
    highest = lax.Precision.HIGHEST
    nt = (((1,), (1,)), ((), ()))

    def full(x):
        return lax.dot_general(x, stretch, nt, precision=highest, preferred_element_type=F32) * same

    fwd = full(jnp.dot(stretch, mmap[...], precision=highest, preferred_element_type=F32))
    bwd = full(lax.dot_general(stretch, mmap[...], nt, precision=highest, preferred_element_type=F32))
    for ref, big in ((map_cat, fwd), (mapt_cat, bwd)):
        high, low = split(big)
        ref[...] = jnp.concatenate(
            [high.astype(F32), low.astype(F32), high.astype(F32)], axis=1
        ).astype(BF)

    timeline[...] = jnp.zeros_like(timeline)
    for i in range(depth):
        timeline[i * PAD : i * PAD + cond, :] = past[0, i]
    damp = jnp.concatenate([att[0], jnp.zeros((PAD - cond, lines), F32)], axis=0)
    span_row = span[...]

    def history(block):
        for t in range(TMIN):
            total = jnp.zeros((PAD, lines), F32)
            for d in range(depth - TMIN + 1):
                at = pl.multiple_of((block * TMIN + t + d) * PAD, PAD)
                total = jnp.where(span_row == depth - d, timeline[pl.ds(at, PAD), :], total)
            hist[t * PAD : (t + 1) * PAD, :] = damp * total

    def start_inject(extra):
        inject = apply_map(map_cat[...], hist[...])
        if extra is not None:
            inject = jnp.where(iota((ROWS, lines), 0) == cond, extra, inject)
        pack(pick(inject, p_hot[...]), inj_send, inj_recv)

    history(0)
    start_inject(local[...].astype(F32))
    pl.semaphore_wait(barrier, n_line - 1 + n_sub - 1)
    for k in range(1, n_line):
        line_copy(inj_send, inj_recv, inj_ss, inj_rs, k).start()

    r, s = iota((2 * ROWS, cond * 128), 0), iota((2 * ROWS, cond * 128), 1)
    spread[...] = (
        ((r // PAD) == ((s & 127) // PAD)) & ((r & (PAD - 1)) == s // 128)
    ).astype(F32).astype(BF)
    expand = (iota((subsets, buses), 0) == iota((subsets, buses), 1) // per).astype(F32).astype(BF)
    count_row = mm(
        jnp.broadcast_to(counts[...].astype(F32), (8, subsets)).astype(BF), expand
    )[0:1]
    slot_in = (iota((1, buses), 1) & (per - 1)).astype(F32)
    live = (slot_in < count_row).astype(F32)
    source[...] = jnp.zeros_like(source)
    for t in range(steps):
        source[t * PAD : t * PAD + cond, :] = src[0, t]
    admit[...] = jnp.concatenate(
        [2.0 * adm[0], jnp.zeros((PAD - cond, lines), F32)] * TMIN, axis=0
    )
    w_copy.wait()

    def relayout(n, carry):
        at = pl.multiple_of(n * (16 * nodes), 128)
        wide = w_flat[:, pl.ds(at, 16 * nodes)]
        cube = jnp.stack([wide[:, i * nodes : (i + 1) * nodes] for i in range(16)], axis=0)
        turned = jnp.transpose(cube, (1, 0, 2))
        high, low = split(turned)
        here = pl.multiple_of(n * 16, 16)
        w_split[:, pl.ds(here, 16), :] = high
        w_split[:, pl.ds(pl.multiple_of(nodes + here, 16), 16), :] = low
        return carry

    lax.fori_loop(0, nodes // 16, relayout, 0)
    partner = lax.bitwise_xor(grp, code[0])

    line_wait(inj_send, inj_recv, inj_ss, inj_rs)
    id_row = unpack(inj_recv)[cond : cond + 1, :]
    qt = (iota((buses, slots), 0).astype(F32) == id_row).astype(F32)
    qt_hot[...] = qt.astype(BF)
    q_hot[...] = qt.T.astype(BF)
    diag = iota((per, 128), 1) & (PAD - 1)

    def one_block(block, carry):
        at = pl.multiple_of(block * ROWS, ROWS)
        summed = pick(unpack(inj_recv), q_hot[...])
        right = (summed + source[pl.ds(at, ROWS), :]) * live
        high, low = split(right)
        both = jnp.concatenate([high.astype(F32), low.astype(F32)], axis=0)
        wide = mm(both.T.astype(BF), spread[...]).astype(BF)
        pieces = []
        for g in range(subsets):
            x = jnp.concatenate(
                [wide[g * per : (g + 1) * per, c * 128 : (c + 1) * 128] for c in range(cond)], axis=0
            )
            y = mm(w_split[g], x)
            y = y[:nodes] + y[nodes:]
            total = jnp.zeros((per, 128), F32)
            for c in range(cond):
                total = jnp.where(diag == c, y[c * per : (c + 1) * per], total)
            pieces.append(total)
        turned = jnp.concatenate(pieces, axis=0).T
        volts = (turned[:ROWS] + turned[ROWS:]) * live
        for t in range(TMIN):
            out[0, block * TMIN + t] = volts[t * PAD : t * PAD + cond]

        @pl.when(block < blocks - 1)
        def _():
            pack(pick(volts, qt_hot[...]), v_send, v_recv)
            for k in range(1, n_line):
                line_copy(v_send, v_recv, v_ss, v_rs, k).start()
            line_wait(v_send, v_recv, v_ss, v_rs)
            modal = apply_map(mapt_cat[...], pick(unpack(v_recv), pt_hot[...]))
            sub_send[...] = admit[...] * modal - hist[...]
            parity = lax.rem(block, 2)
            for k in range(1, n_sub):
                sub_copy(parity, k).start()
            arrived = jnp.zeros((ROWS, lines), F32)
            for k in range(1, n_sub):
                sub_copy(parity, k).wait_recv()
                frm = lax.rem(grp + n_sub - k, n_sub)
                arrived = jnp.where(partner == frm, sub_recv[parity, k - 1], arrived)
            for k in range(1, n_sub):
                sub_copy(parity, k).wait_send()
            timeline[pl.ds(pl.multiple_of((depth + block * TMIN) * PAD, PAD), ROWS), :] = arrived
            history(block + 1)
            start_inject(None)
            for k in range(1, n_line):
                line_copy(inj_send, inj_recv, inj_ss, inj_rs, k).start()
            line_wait(inj_send, inj_recv, inj_ss, inj_rs)

        return carry

    lax.fori_loop(0, blocks, one_block, 0)


def per_device(
    nodal_inverse, bus_source, modal_map, admittance, attenuation, past_waves, tie_code,
    travel_span, bus_owner, bus_local, bus_count,
):
    n_line, n_sub = lax.axis_size("line"), lax.axis_size("sub")
    _, steps, cond, buses = bus_source.shape
    lines = admittance.shape[2]
    depth = past_waves.shape[1]
    subsets = nodal_inverse.shape[1]
    nodes = cond * (buses // subsets)
    cap = 2 * lines // n_line
    slots = n_line * cap
    prow = ROWS * cap // 128
    vmem = pl.BlockSpec(memory_space=pltpu.VMEM)
    smem = pl.BlockSpec(memory_space=pltpu.SMEM)
    dma = pltpu.SemaphoreType.DMA
    return pl.pallas_call(
        functools.partial(kernel, n_line, n_sub),
        out_shape=jax.ShapeDtypeStruct(bus_source.shape, F32),
        in_specs=[pl.BlockSpec(memory_space=pl.ANY), vmem, vmem, vmem, vmem, vmem, smem, vmem,
                  vmem, vmem, vmem],
        out_specs=vmem,
        scratch_shapes=[
            pltpu.VMEM((subsets, nodes * nodes), F32),
            pltpu.VMEM((subsets, 2 * nodes, nodes), BF),
            pltpu.VMEM(((depth + steps) * PAD, lines), F32),
            pltpu.VMEM((lines, slots), BF),
            pltpu.VMEM((slots, lines), BF),
            pltpu.VMEM((slots, buses), BF),
            pltpu.VMEM((buses, slots), BF),
            pltpu.VMEM((2 * ROWS, cond * 128), BF),
            pltpu.VMEM((ROWS, 3 * ROWS), BF),
            pltpu.VMEM((ROWS, 3 * ROWS), BF),
            pltpu.VMEM((steps * PAD, buses), F32),
            pltpu.VMEM((ROWS, lines), F32),
            pltpu.VMEM((ROWS, lines), F32),
            pltpu.VMEM((n_line, prow, 128), F32),
            pltpu.VMEM((n_line, prow, 128), F32),
            pltpu.VMEM((n_line, prow, 128), F32),
            pltpu.VMEM((n_line, prow, 128), F32),
            pltpu.VMEM((ROWS, lines), F32),
            pltpu.VMEM((2, n_sub - 1, ROWS, lines), F32),
            dma,
            dma((n_line,)), dma((n_line,)), dma((n_line,)), dma((n_line,)),
            dma((2, n_sub - 1)), dma((2, n_sub - 1)),
        ],
        compiler_params=pltpu.CompilerParams(
            collective_id=0, has_side_effects=True, vmem_limit_bytes=40 * 1024 * 1024
        ),
    )(
        nodal_inverse, bus_source, modal_map, admittance, attenuation, past_waves, tie_code,
        travel_span, bus_owner[:, :, 0], bus_local, bus_count,
    )


def solution(mesh):
    in_specs = (
        P("sub", "line", None),
        P("sub", None, None, "line"),
        P(),
        P("sub", None, "line"),
        P("sub", None, "line"),
        P("sub", None, None, "line"),
        P("line"),
        P("sub", "line"),
        P("sub", "line", None),
        P("sub", "line"),
        P("sub", "line"),
    )
    out_specs = P("sub", None, None, "line")
    return jax.shard_map(
        per_device, mesh=mesh, in_specs=in_specs, out_specs=out_specs, check_vma=False
    )
```

time: 444 us -> 72.3 us (0.16)
  blocking collectives: 126 us -> 0 us
  local copies, waits for them, and re-layouts: 123 us -> 9.24 us
  other arithmetic: 73.1 us -> 0 us
  Pallas kernels: 0 us -> 62 us
  matrix products: 61.1 us -> 0 us
  starting transfers between devices: 38.9 us -> 0 us
  waiting for transfers between devices: 15.8 us -> 0 us
    all_gather x16 -> x0, blocking collectives: 126 us -> none  [send_each(): everyone = lax.all_gather(outgoing[None], 'sub', axis=0, tiled=True)]
    pallas_call x0 -> x1, Pallas kernels: none -> 62 us  [per_device(): pl.pallas_call(functools.partial(kernel, n_line, n_sub), out_shape=jax.Sh...]
    dot_general x48 -> x0, matrix products: 61.1 us -> none  [the longest x16 42.9 us: solve_buses(): jnp.einsum('gij,gj->gi', square, stacked, precision=lax.Precision.HIGHEST)]
    all_to_all x9 -> x0, starting transfers between devices: 38.9 us -> none  [the longest x4 17.5 us: to_lines(): lax.all_to_all(voltage[:, landed_ids], 'line', split_axis=1, concat_axis=...]
    squeeze x33 -> x0, local copies, waits for them, and re-layouts: 29.9 us -> none  [the longest x16 17.6 us: one_block(): summed[inner]]
    all_to_all x9 -> x0, waiting for transfers between devices: 15.8 us -> none  [the longest x4 15.7 us: to_lines(): lax.all_to_all(voltage[:, landed_ids], 'line', split_axis=1, concat_axis=...]
    scatter-add x4 -> x0, other arithmetic: 15.7 us -> none  [to_buses(): jnp.zeros((rows_here, bus_total), jnp.float32).at[:, landed_ids].add(landed)]
    reshape x64 -> x0, local copies, waits for them, and re-layouts: 13.8 us -> none  [the longest x32 10.5 us: solve_buses(): jnp.transpose(solved.reshape(subsets, conductors, per_subset), (1, 0, 2))]
  transfers between devices with their start and end apart: 9 -> 0, of which waited for: 5 -> 0; matrix products, arithmetic and copies ran while one was open for 12% -> 0% of each run, Pallas kernels for 0% -> 0%
where the time goes in v1:
time: 72.3 us; the launch traced here: 71.9 us
  Pallas kernels  62 us (86%)
  local copies, waits for them, and re-layouts  9.24 us (13%)
    pallas_call x1, Pallas kernels, per_device(): pl.pallas_call(functools.partial(kernel, n_line, n_sub), out_shape=jax.Sh...  62 us
    unnamed x16, local copies, waits for them, and re-layouts  8.44 us

profile of v1, /device:TPU:0, one launch (start us, length us, event | category | flops | bytes accessed | tf_op | source)
XLA Modules:
  0.0 71.9 jit_solution(3144995551476614019)
XLA Ops:
  0.7 0.7 copy.13.adm
  1.4 0.7 copy.14.att
  2.1 0.9 %copy.15.past = f32[1,12,12,256]{3,2,1,0:T(8,128)S(1)} copy(f32[1,12,12,256]{3,0,2,1:T(1,128)} %param.16) | data formatting | bytes 294912 | tf_op args[5]
  3.0 1.0 %copy.12.src = f32[1,16,12,256]{3,2,1,0:T(8,128)S(1)} copy(f32[1,16,12,256]{3,1,2,0:T(8,128)} %param.12) | data formatting | bytes 393216 | tf_op args[1]
  4.1 0.0 copy-start
  4.1 1.7 %copy-done = f32[1,16,36864]{2,1,0:T(8,128)S(1)} copy-done((f32[1,16,36864]{2,1,0:T(8,128)S(1)}, f32[1,16,36864]{2,1,0:T(8,128)}, u32[]{:S(2)}) %copy-start) | copy-done | bytes 2359320
  5.7 0.0 copy-start.1
  5.7 0.7 copy-done.1
  6.4 0.0 copy-start.2
  6.4 0.7 copy-done.2
  7.1 0.0 copy-start.3
  7.1 0.7 copy-done.3
  7.8 0.0 copy-start.4
  7.8 0.7 copy-done.4
  8.5 0.0 copy-start.5
  8.5 0.7 copy-done.5
  9.1 62.0 %shard_map.109 = f32[1,16,12,256]{3,2,1,0:T(8,128)S(1)} custom-call(f32[1,16,36864]{2,1,0:T(8,128)S(1)} %copy-done, f32[1,16,12,256]{3,2,1,0:T(8,128)S(1)} %copy.12.src, f32[12,12]{1,0:T(8,128)S(1)} %copy-done.1, f32[1,12,256]{2,1,0:T(8,128)S(1)} %copy.13.adm, f32[1,12,256]{2,1,0:T(8,128)S(1)} %copy.14.att, f32[1,12,12,256]{3,2,1,0:T(8,128)S(1)} %copy.15.past, ...), custom_call_target="tpu_custom_call" | custom-call | tf_op jit(solution)/shard_map/pallas_call | solution.py:275
  71.1 0.8 %copy.16 = f32[1,16,12,256]{3,1,2,0:T(8,128)} copy(f32[1,16,12,256]{3,2,1,0:T(8,128)S(1)} %shard_map.109) | data formatting | bytes 393216 | tf_op jit(solution)/shard_map/pallas_call | solution.py:275
Async XLA Ops:
  4.1 1.7 %copy-start = (f32[1,16,36864]{2,1,0:T(8,128)S(1)}, f32[1,16,36864]{2,1,0:T(8,128)}, u32[]{:S(2)}) copy-start(f32[1,16,36864]{2,1,0:T(8,128)} %w_hbm.1) | copy-start | bytes 7077892
  5.7 0.7 copy-start.1
  6.4 0.7 copy-start.2
  7.1 0.7 copy-start.3
  7.8 0.7 copy-start.4
  8.5 0.7 copy-start.5

commit v2 on v1

--- a/solution.py
+++ b/solution.py
@@ -9,7 +9,7 @@
 
 TMIN = 4
 PAD = 16
-ROWS = TMIN * PAD
+WIDE = 64
 BF = jnp.bfloat16
 F32 = jnp.float32
 MESH = pl.DeviceIdType.MESH
@@ -40,14 +40,17 @@
 
 
 def kernel(
-    n_line, n_sub, w_hbm, src, mmap, adm, att, past, code, span, owner, local, counts, out,
+    n_line, n_sub, w_hbm, src_in, mmap_in, adm_in, att_in, past_in, code, span_in, owner_in,
+    local_in, counts_in, out,
+    src, mmap, adm, att, past, span, owner, local, counts, in_sem,
     w_flat, w_split, timeline, p_hot, pt_hot, q_hot, qt_hot, spread, map_cat, mapt_cat,
     source, admit, hist, inj_send, inj_recv, v_send, v_recv, sub_send, sub_recv,
     w_sem, inj_ss, inj_rs, v_ss, v_rs, sub_ss, sub_rs,
 ):
     me = lax.axis_index("line")
     grp = lax.axis_index("sub")
-    steps, cond, buses = src.shape[1:]
+    cond, steps, buses = src.shape[1:]
+    rows = TMIN * cond
     lines = adm.shape[2]
     depth = past.shape[1]
     subsets = w_hbm.shape[1]
@@ -57,7 +60,8 @@
     cap = 2 * lines // n_line
     slots = n_line * cap
     parts = 128 // cap
-    prow = ROWS // parts
+    prow = rows // parts
+    sent = -(-prow // 8) * 8
 
     barrier = pltpu.get_barrier_semaphore()
     for k in range(1, n_line):
@@ -69,37 +73,52 @@
             barrier, inc=1, device_id={"sub": lax.rem(grp + k, n_sub)}, device_id_type=MESH
         )
     w_copy = pltpu.make_async_copy(w_hbm.at[0], w_flat, w_sem)
+    loads = [
+        pltpu.make_async_copy(a, b, in_sem.at[i])
+        for i, (a, b) in enumerate(
+            [(owner_in, owner), (local_in, local), (span_in, span), (mmap_in, mmap), (past_in, past),
+             (att_in, att), (adm_in, adm), (src_in, src), (counts_in, counts)]
+        )
+    ]
+    for load in loads:
+        load.start()
     w_copy.start()
-
-    def line_copy(send, recv, ss, rs, k):
+    for load in loads[:6]:
+        load.wait()
+
+    def line_copy(send, recv, ss, rs, k, high=None):
+        high = sent if high is None else high
         to = lax.rem(me + k, n_line)
         return pltpu.make_async_remote_copy(
-            src_ref=send.at[to], dst_ref=recv.at[me], send_sem=ss.at[k], recv_sem=rs.at[k],
+            src_ref=send.at[to, 0:high], dst_ref=recv.at[me, 0:high], send_sem=ss.at[k], recv_sem=rs.at[k],
             device_id={"line": to}, device_id_type=MESH,
         )
 
-    def line_wait(send, recv, ss, rs):
+    def line_wait(send, recv, ss, rs, high=None):
+        high = sent if high is None else high
         for k in range(1, n_line):
             frm = lax.rem(me + n_line - k, n_line)
             pltpu.make_async_remote_copy(
-                src_ref=send.at[frm], dst_ref=recv.at[frm], send_sem=ss.at[k], recv_sem=rs.at[k],
+                src_ref=send.at[frm, 0:high], dst_ref=recv.at[frm, 0:high], send_sem=ss.at[k], recv_sem=rs.at[k],
                 device_id={"line": frm}, device_id_type=MESH,
             ).wait_recv()
+
+    def line_sent(send, recv, ss, rs, high=None):
         for k in range(1, n_line):
-            line_copy(send, recv, ss, rs, k).wait_send()
+            line_copy(send, recv, ss, rs, k, high).wait_send()
 
     def pack(x, send, recv):
         for d in range(n_line):
-            send[d] = jnp.concatenate(
+            send[d, 0:prow] = jnp.concatenate(
                 [x[g * prow : (g + 1) * prow, d * cap : (d + 1) * cap] for g in range(parts)], axis=1
             )
-        recv[me] = send[me]
+        recv[me, 0:prow] = send[me, 0:prow]
 
     def unpack(recv):
         return jnp.concatenate(
             [
                 jnp.concatenate(
-                    [recv[d][:, g * cap : (g + 1) * cap] for d in range(n_line)], axis=1
+                    [recv[d, 0:prow][:, g * cap : (g + 1) * cap] for d in range(n_line)], axis=1
                 )
                 for g in range(parts)
             ],
@@ -122,8 +141,8 @@
     pt_hot[...] = pt.astype(BF)
     p_hot[...] = pt.T.astype(BF)
 
-    stretch = ((iota((ROWS, cond), 0) & (PAD - 1)) == iota((ROWS, cond), 1)).astype(F32)
-    same = (iota((ROWS, ROWS), 0) // PAD == iota((ROWS, ROWS), 1) // PAD).astype(F32)
+    stretch = (iota((rows, cond), 0) % cond == iota((rows, cond), 1)).astype(F32)
+    same = (iota((rows, rows), 0) // cond == iota((rows, rows), 1) // cond).astype(F32)
     highest = lax.Precision.HIGHEST
     nt = (((1,), (1,)), ((), ()))
 
@@ -150,23 +169,38 @@
             for d in range(depth - TMIN + 1):
                 at = pl.multiple_of((block * TMIN + t + d) * PAD, PAD)
                 total = jnp.where(span_row == depth - d, timeline[pl.ds(at, PAD), :], total)
-            hist[t * PAD : (t + 1) * PAD, :] = damp * total
+            hist[t * cond : (t + 1) * cond, :] = (damp * total)[:cond]
 
     def start_inject(extra):
         inject = apply_map(map_cat[...], hist[...])
         if extra is not None:
-            inject = jnp.where(iota((ROWS, lines), 0) == cond, extra, inject)
-        pack(pick(inject, p_hot[...]), inj_send, inj_recv)
+            both = jnp.concatenate([inject, jnp.broadcast_to(extra, (16, lines))], axis=0)
+            both = pick(both, p_hot[...])
+            inject = both[:rows]
+            for d in range(n_line):
+                piece = both[rows : rows + 8, d * cap : (d + 1) * cap]
+                inj_send[d, sent : sent + 8] = jnp.concatenate([piece] * parts, axis=1)
+            inj_recv[me, sent : sent + 8] = inj_send[me, sent : sent + 8]
+        else:
+            inject = pick(inject, p_hot[...])
+        pack(inject, inj_send, inj_recv)
 
     history(0)
+    if sent > prow:
+        inj_send[...] = jnp.zeros_like(inj_send)
+        v_send[...] = jnp.zeros_like(v_send)
     start_inject(local[...].astype(F32))
     pl.semaphore_wait(barrier, n_line - 1 + n_sub - 1)
     for k in range(1, n_line):
-        line_copy(inj_send, inj_recv, inj_ss, inj_rs, k).start()
-
-    r, s = iota((2 * ROWS, cond * 128), 0), iota((2 * ROWS, cond * 128), 1)
+        line_copy(inj_send, inj_recv, inj_ss, inj_rs, k, sent + 8).start()
+
+    for load in loads[6:]:
+        load.wait()
+    r, s = iota((2 * WIDE, cond * 128), 0), iota((2 * WIDE, cond * 128), 1)
+    r_in, s_in = r & (WIDE - 1), s & (WIDE - 1)
     spread[...] = (
-        ((r // PAD) == ((s & 127) // PAD)) & ((r & (PAD - 1)) == s // 128)
+        (r // WIDE == (s & 127) // WIDE) & (r_in // cond == s_in // cond)
+        & (r_in % cond == s // 128)
     ).astype(F32).astype(BF)
     expand = (iota((subsets, buses), 0) == iota((subsets, buses), 1) // per).astype(F32).astype(BF)
     count_row = mm(
@@ -174,12 +208,9 @@
     )[0:1]
     slot_in = (iota((1, buses), 1) & (per - 1)).astype(F32)
     live = (slot_in < count_row).astype(F32)
-    source[...] = jnp.zeros_like(source)
     for t in range(steps):
-        source[t * PAD : t * PAD + cond, :] = src[0, t]
-    admit[...] = jnp.concatenate(
-        [2.0 * adm[0], jnp.zeros((PAD - cond, lines), F32)] * TMIN, axis=0
-    )
+        source[t * cond : (t + 1) * cond, :] = src[0, :, t, :]
+    admit[...] = jnp.concatenate([2.0 * adm[0]] * TMIN, axis=0)
     w_copy.wait()
 
     def relayout(n, carry):
@@ -196,19 +227,23 @@
     lax.fori_loop(0, nodes // 16, relayout, 0)
     partner = lax.bitwise_xor(grp, code[0])
 
-    line_wait(inj_send, inj_recv, inj_ss, inj_rs)
-    id_row = unpack(inj_recv)[cond : cond + 1, :]
+    line_wait(inj_send, inj_recv, inj_ss, inj_rs, sent + 8)
+    line_sent(inj_send, inj_recv, inj_ss, inj_rs, sent + 8)
+    id_row = jnp.concatenate(
+        [inj_recv[d, sent : sent + 8][0:1, 0:cap] for d in range(n_line)], axis=1
+    )
     qt = (iota((buses, slots), 0).astype(F32) == id_row).astype(F32)
     qt_hot[...] = qt.astype(BF)
     q_hot[...] = qt.T.astype(BF)
-    diag = iota((per, 128), 1) & (PAD - 1)
+    diag = (iota((per, 128), 1) & (WIDE - 1)) % cond
 
     def one_block(block, carry):
-        at = pl.multiple_of(block * ROWS, ROWS)
+        at = pl.multiple_of(block * rows, 8)
         summed = pick(unpack(inj_recv), q_hot[...])
-        right = (summed + source[pl.ds(at, ROWS), :]) * live
+        right = (summed + source[pl.ds(at, rows), :]) * live
         high, low = split(right)
-        both = jnp.concatenate([high.astype(F32), low.astype(F32)], axis=0)
+        gap = jnp.zeros((WIDE - rows, buses), F32)
+        both = jnp.concatenate([high.astype(F32), gap, low.astype(F32), gap], axis=0)
         wide = mm(both.T.astype(BF), spread[...]).astype(BF)
         pieces = []
         for g in range(subsets):
@@ -222,9 +257,9 @@
                 total = jnp.where(diag == c, y[c * per : (c + 1) * per], total)
             pieces.append(total)
         turned = jnp.concatenate(pieces, axis=0).T
-        volts = (turned[:ROWS] + turned[ROWS:]) * live
+        volts = (turned[:rows] + turned[WIDE : WIDE + rows]) * live
         for t in range(TMIN):
-            out[0, block * TMIN + t] = volts[t * PAD : t * PAD + cond]
+            out[0, block * TMIN + t] = volts[t * cond : (t + 1) * cond]
 
         @pl.when(block < blocks - 1)
         def _():
@@ -237,19 +272,26 @@
             parity = lax.rem(block, 2)
             for k in range(1, n_sub):
                 sub_copy(parity, k).start()
-            arrived = jnp.zeros((ROWS, lines), F32)
+            arrived = jnp.zeros((rows, lines), F32)
             for k in range(1, n_sub):
                 sub_copy(parity, k).wait_recv()
                 frm = lax.rem(grp + n_sub - k, n_sub)
                 arrived = jnp.where(partner == frm, sub_recv[parity, k - 1], arrived)
-            for k in range(1, n_sub):
-                sub_copy(parity, k).wait_send()
-            timeline[pl.ds(pl.multiple_of((depth + block * TMIN) * PAD, PAD), ROWS), :] = arrived
+            gap = jnp.zeros((PAD - cond, lines), F32)
+            for t in range(TMIN):
+                here = pl.multiple_of((depth + block * TMIN + t) * PAD, PAD)
+                timeline[pl.ds(here, PAD), :] = jnp.concatenate(
+                    [arrived[t * cond : (t + 1) * cond], gap], axis=0
+                )
             history(block + 1)
             start_inject(None)
             for k in range(1, n_line):
                 line_copy(inj_send, inj_recv, inj_ss, inj_rs, k).start()
+            line_sent(v_send, v_recv, v_ss, v_rs)
+            for k in range(1, n_sub):
+                sub_copy(parity, k).wait_send()
             line_wait(inj_send, inj_recv, inj_ss, inj_rs)
+            line_sent(inj_send, inj_recv, inj_ss, inj_rs)
 
         return carry
 
@@ -268,17 +310,28 @@
     nodes = cond * (buses // subsets)
     cap = 2 * lines // n_line
     slots = n_line * cap
-    prow = ROWS * cap // 128
+    rows = TMIN * cond
+    sent = -(-(rows * cap // 128) // 8) * 8
     vmem = pl.BlockSpec(memory_space=pltpu.VMEM)
+    hbm = pl.BlockSpec(memory_space=pl.ANY)
     smem = pl.BlockSpec(memory_space=pltpu.SMEM)
     dma = pltpu.SemaphoreType.DMA
     return pl.pallas_call(
         functools.partial(kernel, n_line, n_sub),
         out_shape=jax.ShapeDtypeStruct(bus_source.shape, F32),
-        in_specs=[pl.BlockSpec(memory_space=pl.ANY), vmem, vmem, vmem, vmem, vmem, smem, vmem,
-                  vmem, vmem, vmem],
+        in_specs=[hbm] * 6 + [smem] + [hbm] * 4,
         out_specs=vmem,
         scratch_shapes=[
+            pltpu.VMEM((1, cond, steps, buses), F32),
+            pltpu.VMEM((cond, cond), F32),
+            pltpu.VMEM((1, cond, lines), F32),
+            pltpu.VMEM((1, cond, lines), F32),
+            pltpu.VMEM((1, depth, cond, lines), F32),
+            pltpu.VMEM((1, lines), jnp.int32),
+            pltpu.VMEM((1, lines), jnp.int32),
+            pltpu.VMEM((1, lines), jnp.int32),
+            pltpu.VMEM((1, subsets), jnp.int32),
+            dma((9,)),
             pltpu.VMEM((subsets, nodes * nodes), F32),
             pltpu.VMEM((subsets, 2 * nodes, nodes), BF),
             pltpu.VMEM(((depth + steps) * PAD, lines), F32),
@@ -286,28 +339,28 @@
             pltpu.VMEM((slots, lines), BF),
             pltpu.VMEM((slots, buses), BF),
             pltpu.VMEM((buses, slots), BF),
-            pltpu.VMEM((2 * ROWS, cond * 128), BF),
-            pltpu.VMEM((ROWS, 3 * ROWS), BF),
-            pltpu.VMEM((ROWS, 3 * ROWS), BF),
-            pltpu.VMEM((steps * PAD, buses), F32),
-            pltpu.VMEM((ROWS, lines), F32),
-            pltpu.VMEM((ROWS, lines), F32),
-            pltpu.VMEM((n_line, prow, 128), F32),
-            pltpu.VMEM((n_line, prow, 128), F32),
-            pltpu.VMEM((n_line, prow, 128), F32),
-            pltpu.VMEM((n_line, prow, 128), F32),
-            pltpu.VMEM((ROWS, lines), F32),
-            pltpu.VMEM((2, n_sub - 1, ROWS, lines), F32),
+            pltpu.VMEM((2 * WIDE, cond * 128), BF),
+            pltpu.VMEM((rows, 3 * rows), BF),
+            pltpu.VMEM((rows, 3 * rows), BF),
+            pltpu.VMEM((steps * cond, buses), F32),
+            pltpu.VMEM((rows, lines), F32),
+            pltpu.VMEM((rows, lines), F32),
+            pltpu.VMEM((n_line, sent + 8, 128), F32),
+            pltpu.VMEM((n_line, sent + 8, 128), F32),
+            pltpu.VMEM((n_line, sent, 128), F32),
+            pltpu.VMEM((n_line, sent, 128), F32),
+            pltpu.VMEM((rows, lines), F32),
+            pltpu.VMEM((2, n_sub - 1, rows, lines), F32),
             dma,
             dma((n_line,)), dma((n_line,)), dma((n_line,)), dma((n_line,)),
             dma((2, n_sub - 1)), dma((2, n_sub - 1)),
         ],
         compiler_params=pltpu.CompilerParams(
-            collective_id=0, has_side_effects=True, vmem_limit_bytes=40 * 1024 * 1024
+            collective_id=0, has_side_effects=True, vmem_limit_bytes=56 * 1024 * 1024
         ),
     )(
-        nodal_inverse, bus_source, modal_map, admittance, attenuation, past_waves, tie_code,
-        travel_span, bus_owner[:, :, 0], bus_local, bus_count,
+        nodal_inverse, jnp.transpose(bus_source, (0, 2, 1, 3)), modal_map, admittance, attenuation,
+        past_waves, tie_code, travel_span, bus_owner[:, :, 0], bus_local, bus_count,
     )
 
 

time: 72.3 us -> 64.7 us (0.89)
  Pallas kernels: 62 us -> 57.8 us
  local copies, waits for them, and re-layouts: 9.24 us -> 5.96 us
    unnamed x16 -> x3, local copies, waits for them, and re-layouts: 8.44 us -> 4.22 us
    pallas_call x1, Pallas kernels: 62 us -> 57.8 us  [per_device(): pl.pallas_call(functools.partial(kernel, n_line, n_sub), out_shape=jax.Sh...]
    pallas_call x1, local copies, waits for them, and re-layouts: 0.8 us -> 1.75 us  [per_device(): pl.pallas_call(functools.partial(kernel, n_line, n_sub), out_shape=jax.Sh...]
where the time goes in v2:
time: 64.7 us; the launch traced here: 64.4 us
  Pallas kernels  57.8 us (89%)
  local copies, waits for them, and re-layouts  5.96 us (9%)
  between operations  0.66 us (1%)
    pallas_call x1, Pallas kernels, per_device(): pl.pallas_call(functools.partial(kernel, n_line, n_sub), out_shape=jax.Sh...  57.8 us
    unnamed x3, local copies, waits for them, and re-layouts  4.22 us
    pallas_call x1, local copies, waits for them, and re-layouts, per_device(): pl.pallas_call(functools.partial(kernel, n_line, n_sub), out_shape=jax.Sh...  1.75 us

profile of v2, /device:TPU:0, one launch (start us, length us, event | category | flops | bytes accessed | tf_op | source)
XLA Modules:
  0.0 64.4 jit_solution(5845560528759676058)
XLA Ops:
  0.7 1.3 %copy.12.adm_in = f32[1,12,256]{2,1,0:T(8,128)} copy(f32[1,12,256]{2,0,1:T(1,128)} %param.14) | data formatting | bytes 24576 | tf_op args[3]
  2.0 1.3 %copy.13.att_in = f32[1,12,256]{2,1,0:T(8,128)} copy(f32[1,12,256]{2,0,1:T(1,128)} %param.15) | data formatting | bytes 24576 | tf_op args[4]
  3.3 1.6 %copy.14.past_in = f32[1,12,12,256]{3,2,1,0:T(8,128)} copy(f32[1,12,12,256]{3,0,2,1:T(1,128)} %param.16) | data formatting | bytes 294912 | tf_op args[5]
  4.9 57.8 %shard_map.109 = f32[1,16,12,256]{3,2,1,0:T(8,128)} custom-call(f32[1,16,36864]{2,1,0:T(8,128)} %w_hbm.1, f32[1,12,16,256]{3,2,1,0:T(8,128)} %bitcast.2, f32[12,12]{1,0:T(8,128)} %mmap_in.1, f32[1,12,256]{2,1,0:T(8,128)} %copy.12.adm_in, f32[1,12,256]{2,1,0:T(8,128)} %copy.13.att_in, f32[1,12,12,256]{3,2,1,0:T(8,128)} %copy.14.past_in, s32[1]{0:T(128)S(6)} %copy.16.code, ...), custom_call_target="tpu_custom_call" | custom-call | tf_op jit(solution)/shard_map/pallas_call | solution.py:319
  62.7 1.7 %copy.15 = f32[1,16,12,256]{3,1,2,0:T(8,128)} copy(f32[1,16,12,256]{3,2,1,0:T(8,128)} %shard_map.109) | data formatting | bytes 393216 | tf_op jit(solution)/shard_map/pallas_call | solution.py:319

commit v3 on v2

--- a/solution.py
+++ b/solution.py
@@ -52,7 +52,7 @@
     cond, steps, buses = src.shape[1:]
     rows = TMIN * cond
     lines = adm.shape[2]
-    depth = past.shape[1]
+    depth = past.shape[0]
     subsets = w_hbm.shape[1]
     per = buses // subsets
     nodes = cond * per
@@ -150,17 +150,18 @@
         return lax.dot_general(x, stretch, nt, precision=highest, preferred_element_type=F32) * same
 
     fwd = full(jnp.dot(stretch, mmap[...], precision=highest, preferred_element_type=F32))
-    bwd = full(lax.dot_general(stretch, mmap[...], nt, precision=highest, preferred_element_type=F32))
-    for ref, big in ((map_cat, fwd), (mapt_cat, bwd)):
+
+    def three(big):
         high, low = split(big)
-        ref[...] = jnp.concatenate(
+        return jnp.concatenate(
             [high.astype(F32), low.astype(F32), high.astype(F32)], axis=1
         ).astype(BF)
 
-    timeline[...] = jnp.zeros_like(timeline)
+    map_cat[...] = three(fwd)
+
     for i in range(depth):
-        timeline[i * PAD : i * PAD + cond, :] = past[0, i]
-    damp = jnp.concatenate([att[0], jnp.zeros((PAD - cond, lines), F32)], axis=0)
+        timeline[i * PAD : i * PAD + cond, :] = past[i, :, 0, :]
+    damp = jnp.concatenate([att[:, 0, :], jnp.zeros((PAD - cond, lines), F32)], axis=0)
     span_row = span[...]
 
     def history(block):
@@ -196,6 +197,9 @@
 
     for load in loads[6:]:
         load.wait()
+    mapt_cat[...] = three(
+        full(lax.dot_general(stretch, mmap[...], nt, precision=highest, preferred_element_type=F32))
+    )
     r, s = iota((2 * WIDE, cond * 128), 0), iota((2 * WIDE, cond * 128), 1)
     r_in, s_in = r & (WIDE - 1), s & (WIDE - 1)
     spread[...] = (
@@ -210,7 +214,7 @@
     live = (slot_in < count_row).astype(F32)
     for t in range(steps):
         source[t * cond : (t + 1) * cond, :] = src[0, :, t, :]
-    admit[...] = jnp.concatenate([2.0 * adm[0]] * TMIN, axis=0)
+    admit[...] = jnp.concatenate([2.0 * adm[:, 0, :]] * TMIN, axis=0)
     w_copy.wait()
 
     def relayout(n, carry):
@@ -324,9 +328,9 @@
         scratch_shapes=[
             pltpu.VMEM((1, cond, steps, buses), F32),
             pltpu.VMEM((cond, cond), F32),
-            pltpu.VMEM((1, cond, lines), F32),
-            pltpu.VMEM((1, cond, lines), F32),
-            pltpu.VMEM((1, depth, cond, lines), F32),
+            pltpu.VMEM((cond, 1, lines), F32),
+            pltpu.VMEM((cond, 1, lines), F32),
+            pltpu.VMEM((depth, cond, 1, lines), F32),
             pltpu.VMEM((1, lines), jnp.int32),
             pltpu.VMEM((1, lines), jnp.int32),
             pltpu.VMEM((1, lines), jnp.int32),
@@ -359,8 +363,9 @@
             collective_id=0, has_side_effects=True, vmem_limit_bytes=56 * 1024 * 1024
         ),
     )(
-        nodal_inverse, jnp.transpose(bus_source, (0, 2, 1, 3)), modal_map, admittance, attenuation,
-        past_waves, tie_code, travel_span, bus_owner[:, :, 0], bus_local, bus_count,
+        nodal_inverse, jnp.transpose(bus_source, (0, 2, 1, 3)), modal_map,
+        jnp.transpose(admittance, (1, 0, 2)), jnp.transpose(attenuation, (1, 0, 2)),
+        jnp.transpose(past_waves, (1, 2, 0, 3)), tie_code, travel_span, bus_owner[:, :, 0], bus_local, bus_count,
     )
 
 

time: 64.7 us -> 60.4 us (0.934)
  local copies, waits for them, and re-layouts: 5.96 us -> 1.75 us
    unnamed x3 -> x0, local copies, waits for them, and re-layouts: 4.22 us -> none
where the time goes in v3:
time: 60.4 us; the launch traced here: 60.2 us
  Pallas kernels  57.8 us (96%)
  local copies, waits for them, and re-layouts  1.75 us (3%)
  between operations  0.66 us (1%)
    pallas_call x1, Pallas kernels, per_device(): pl.pallas_call(functools.partial(kernel, n_line, n_sub), out_shape=jax.Sh...  57.8 us
    pallas_call x1, local copies, waits for them, and re-layouts, per_device(): pl.pallas_call(functools.partial(kernel, n_line, n_sub), out_shape=jax.Sh...  1.75 us

profile of v3, /device:TPU:0, one launch (start us, length us, event | category | flops | bytes accessed | tf_op | source)
XLA Modules:
  0.0 60.2 jit_solution(17874958734377758022)
XLA Ops:
  0.7 57.8 %shard_map.109 = f32[1,16,12,256]{3,2,1,0:T(8,128)} custom-call(f32[1,16,36864]{2,1,0:T(8,128)} %w_hbm.1, f32[1,12,16,256]{3,2,1,0:T(8,128)} %bitcast.5, f32[12,12]{1,0:T(8,128)} %mmap_in.1, f32[12,1,256]{2,1,0:T(1,128)} %bitcast.7, f32[12,1,256]{2,1,0:T(1,128)} %bitcast.8, f32[12,12,1,256]{3,2,1,0:T(1,128)} %bitcast.6, s32[1]{0:T(128)S(6)} %copy.13.code, ...), custom_call_target="tpu_custom_call" | custom-call | tf_op jit(solution)/shard_map/pallas_call | solution.py:323
  58.5 1.7 %copy.12 = f32[1,16,12,256]{3,1,2,0:T(8,128)} copy(f32[1,16,12,256]{3,2,1,0:T(8,128)} %shard_map.109) | data formatting | bytes 393216 | tf_op jit(solution)/shard_map/pallas_call | solution.py:323
